TPU v7x, 32 devices: a whole 2x2x4 slice. The times are simulated.
32 devices in a mesh: ia: 4 (over y, x), ja: 8 (over z, core).
Axes of the slice: x: 2, y: 2, z: 4, core: 2. Of those that a mesh axis runs over, the one named last changes fastest.
Arguments:
- phase_space: float32 [12, 8192], P(None, 'ja'), may hold values from -6 to 6
- star_mass: float32 [8192], P('ja'), may hold values from 6.1035156e-05 to 0.00024414062
- star_level: int32 [8192], P('ja'), may hold values from 0 to 3
- active_ids: int32 [2, 64, 128], P(None, 'ia'), may hold values from 0 to 8191, as said below
- active_counts: int32 [2, 64], P(None, 'ia'), may hold values from 1 to 128, as said below
Outputs:
- final_state: float32 [12, 8192], P(None, 'ja')
- active_force: float32 [2, 6, 8192], P(None, None, ('ia', 'ja'))
Inputs may be any that keep to these rules, and one draw needn't show every extreme that they name: `active_ids`: within one block step the 64 x 128 entries are distinct star numbers; entries of unused slots are ignored. `active_counts`: in every block step one block is full and one holds a single star.
All inputs are finite; a program needn't handle non-finite values.
Results may differ from a plain program's by a relative error of at most 0.00018.
Values sent between devices are 32-bit elements; how exact they have to be, the bound alone decides.
A program may use at most 64 MiB of HBM per device.

v0:
```python
import jax
import jax.numpy as jnp
from jax import lax
from jax.sharding import PartitionSpec as P

STEPS = 2
EPS2 = 0.01
STEP_TIME = 0.05


def predict(state, tau):
    tau_sq = tau * tau
    tau_cube = tau_sq * tau
    new_pos = (
        state[0:3] + state[3:6] * tau + state[6:9] * (tau_sq * 0.5) + state[9:12] * (tau_cube / 6.0)
    )
    new_vel = state[3:6] + state[6:9] * tau + state[9:12] * (tau_sq * 0.5)
    return (new_pos, new_vel)


def field_force(target_pos, target_vel, source_pos, source_vel, source_mass):
    offset = source_pos[:, None, :] - target_pos[:, :, None]
    rel_vel = source_vel[:, None, :] - target_vel[:, :, None]
    dist_sq = jnp.sum(offset * offset, axis=0) + EPS2
    inverse = lax.rsqrt(dist_sq)
    weight = source_mass[None, :] * inverse * inverse * inverse
    radial = 3.0 * jnp.sum(offset * rel_vel, axis=0) / dist_sq
    accel = jnp.sum(weight[None] * offset, axis=2)
    jolt = jnp.sum(weight[None] * (rel_vel - radial[None] * offset), axis=2)
    return jnp.concatenate([accel, jolt], axis=0)


def blocked_force(target_pos, target_vel, source_pos, source_vel, source_mass, block_rows):
    total_rows = target_pos.shape[1]
    block_count = total_rows // block_rows
    tiles = (
        target_pos.reshape(3, block_count, block_rows).transpose(1, 0, 2),
        target_vel.reshape(3, block_count, block_rows).transpose(1, 0, 2),
    )

    def one_tile(pair_tile):
        return field_force(pair_tile[0], pair_tile[1], source_pos, source_vel, source_mass)

    result = lax.map(one_tile, tiles)
    return result.transpose(1, 0, 2).reshape(6, total_rows)


def correct(active_rows, accel, jolt, span):
    half_step = span * 0.5
    twelfth = span * span / 12.0
    old_pos = active_rows[0:3]
    old_vel = active_rows[3:6]
    old_acc = active_rows[6:9]
    old_jerk = active_rows[9:12]
    new_vel = old_vel + (old_acc + accel) * half_step + (old_jerk - jolt) * twelfth
    new_pos = old_pos + (old_vel + new_vel) * half_step + (old_acc - accel) * twelfth
    return jnp.concatenate([new_pos, new_vel, accel, jolt], axis=0)


def local(phase_space, star_mass, star_level, active_ids, active_counts):
    shard_width = phase_space.shape[1]
    shard_start = lax.axis_index("ja") * shard_width
    block_rows = 512
    state = phase_space
    last = -STEP_TIME * star_level.astype(jnp.float32)
    force_steps = []
    for step_index in range(STEPS):
        clock = STEP_TIME * (step_index + 1)
        indices = active_ids[step_index].reshape(-1)
        slot_pos = lax.broadcasted_iota(jnp.int32, (active_ids.shape[1], active_ids.shape[2]), 1)
        usable = (slot_pos < active_counts[step_index][:, None]).reshape(-1)
        local_ids = indices - shard_start
        inside = (local_ids >= 0) & (local_ids < shard_width)
        clipped = jnp.clip(local_ids, 0, shard_width - 1)
        fpos, fvel = predict(state, clock - last)
        stacked = jnp.concatenate([state, last[None, :]], axis=0)
        picked = jnp.where(inside[None, :], jnp.take(stacked, clipped, axis=1), 0.0)
        target_state = lax.psum(picked, "ja")
        tpos, tvel = predict(target_state[0:12], clock - target_state[12])
        partial_value = blocked_force(tpos, tvel, fpos, fvel, star_mass, block_rows)
        write_ids = jnp.where(usable, indices, -1)
        forces = lax.psum(partial_value, "ja")
        share_len = forces.shape[1] // lax.axis_size("ja")
        share_start = lax.axis_index("ja") * share_len
        force_share = lax.dynamic_slice_in_dim(forces, share_start, share_len, 1)
        usable_share = lax.dynamic_slice_in_dim(usable, share_start, share_len, 0)
        force_steps.append(jnp.where(usable_share[None, :], force_share, 0.0))
        outgoing = correct(target_state[0:12], forces[0:3], forces[3:6], clock - target_state[12])
        returned, return_ids = (
            lax.all_gather(outgoing, "ia", axis=1, tiled=True),
            lax.all_gather(write_ids, "ia", axis=0, tiled=True),
        )
        placed_raw = return_ids - shard_start
        valid = (return_ids >= 0) & (placed_raw >= 0) & (placed_raw < shard_width)
        placed = jnp.where(valid, placed_raw, shard_width)
        state = state.at[:, placed].set(returned, mode="drop")
        last = last.at[placed].set(clock, mode="drop")
    return (state, jnp.stack(force_steps))


def solution(mesh):
    placed = (P(None, "ja"), P("ja"), P("ja"), P(None, "ia", None), P(None, "ia"))
    return jax.shard_map(
        local,
        mesh=mesh,
        in_specs=placed,
        out_specs=(P(None, "ja"), P(None, None, ("ia", "ja"))),
        check_vma=False,
    )
```

profile of v0, /device:TPU:0, one launch (start us, length us, event | category | flops | bytes accessed | tf_op | source)
XLA Modules:
  0.0 312.5 jit_solution(17012939076392843902)
XLA Ops:
  11.3 5.5 %gather_fusion = f32[2048,13]{1,0:T(8,128)S(1)} fusion(f32[13,1024]{0,1:T(8,128)S(1)} %copy.110, s32[2048]{0:T(1024)S(1)} %get-tuple-element.164), kind=kCustom, calls=%fused_computation.clone | custom fusion | bytes 221184 | tf_op jit(solution)/shard_map/jit(_take)/gather | solution.py:77
  17.9 9.6 %all_gather.14 = s32[8192]{0:T(1024)S(1)} all-gather(s32[2048]{0:T(1024)S(1)} %get-tuple-element.165), channel_id=1, replica_groups=mesh['ia'=4,'ja'=8] {'ia'}, dimensions={0}, use_global_device_ids=true | all-gather | bytes 40960 | tf_op jit(solution)/shard_map/all_gather | solution.py:91
  27.5 8.1 %all_gather.12 = s32[8192]{0:T(1024)S(1)} all-gather(s32[2048]{0:T(1024)S(1)} %get-tuple-element.166), channel_id=1, replica_groups=mesh['ia'=4,'ja'=8] {'ia'}, dimensions={0}, use_global_device_ids=true | all-gather | bytes 40960 | tf_op jit(solution)/shard_map/all_gather | solution.py:91
  35.7 30.4 %scatter_fusion.1 = f32[1024]{0:T(1024)S(1)} fusion(f32[1024]{0:T(1024)S(1)} %get-tuple-element.170, s32[8192]{0:T(1024)S(1)} %compare_select_fusion.1, f32[8192]{0:T(1024)S(1)} %broadcast.175), kind=kCustom, calls=%fused_computation.3 | custom fusion | bytes 131072 | tf_op jit(solution)/shard_map/scatter | solution.py:97
  66.9 7.9 %all-reduce.3.cloned.1.call-done = f32[13,2048]{1,0:T(8,128)} async-done(((f32[13,2048]{1,0:T(8,128)}), f32[13,2048]{1,0:T(8,128)}) %all-reduce.3.cloned.1.call-update) | async-done | bytes 106512 | tf_op jit(solution)/shard_map/psum | solution.py:78
  74.8 0.9 broadcast_multiply_fusion.1
  75.7 1.0 multiply_add_fusion.4
  76.8 20.9 %while.20 = (s32[]{:T(128)}, f32[4,6,512]{2,1,0:T(8,128)S(1)}, f32[1024]{0:T(1024)S(1)}, f32[3,1024]{1,0:T(4,128)S(1)}, f32[4,3,512]{2,1,0:T(4,128)S(1)}, /*inde...) while((s32[]{:T(128)}, f32[4,6,512]{2,1,0:T(8,128)S(1)}, f32[1024]{0:T(1024)S(1)}, ...), condition=%wide.region_6.8_spmd, body=%wide.region_1.7_spmd.sunk | while | flops 24117248 | bytes 16924772 | solution.py:44
  76.8 1.8 fusion.31
  78.6 0.9 multiply_divide_fusion.4
  79.5 2.4 fusion.32
  82.0 1.8 fusion.31
  83.8 0.9 multiply_divide_fusion.4
  84.8 2.4 fusion.32
  87.2 1.8 fusion.31
  89.0 0.9 multiply_divide_fusion.4
  90.0 2.4 fusion.32
  92.5 1.8 fusion.31
  94.3 0.9 multiply_divide_fusion.4
  95.2 2.4 fusion.32
  97.7 26.3 %psum.29 = f32[6,2048]{1,0:T(8,128)S(1)} all-reduce(f32[6,2048]{1,0:T(8,128)S(1)} %bitcast.106), channel_id=1, replica_groups=mesh['ia'=4,'ja'=8] {'ja'}, use_global_device_ids=true, to_apply=%region_7.9 | all-reduce | flops 12288 | bytes 98304 | tf_op jit(solution)/shard_map/psum | solution.py:82
  124.1 10.0 %all_gather.13 = f32[12,8192]{1,0:T(8,128)S(1)} all-gather(f32[12,2048]{1,0:T(8,128)S(1)} %pad_maximum_fusion.1), channel_id=1, replica_groups=mesh['ia'=4,'ja'=8] {'ia'}, dimensions={1}, use_global_device_ids=true | all-gather | bytes 491520 | tf_op jit(solution)/shard_map/all_gather | solution.py:90
  134.1 2.6 copy.115
  136.8 21.2 %scatter_fusion = f32[12,1024]{0,1:T(8,128)S(1)} fusion(f32[12,1024]{0,1:T(8,128)S(1)} %copy.114, s32[8192]{0:T(1024)S(1)} %compare_select_fusion.1, f32[8192,12]{1,0:T(8,128)} %copy.115), kind=kCustom, calls=%fused_computation.2 | custom fusion | bytes 1212416 | tf_op jit(solution)/shard_map/scatter | solution.py:96
  158.0 1.3 fusion.24
  159.5 7.6 %gather_fusion.1 = f32[2048,13]{1,0:T(8,128)} fusion(f32[13,1024]{0,1:T(8,128)S(1)} %pad_maximum_fusion, s32[2048]{0:T(1024)S(1)} %get-tuple-element.163), kind=kCustom, calls=%fused_computation.1.clone | custom fusion | bytes 221184 | tf_op jit(solution)/shard_map/jit(_take)/gather | solution.py:77
  167.1 1.6 copy.117
  169.3 1.2 copy.129
  171.2 50.0 %all-reduce.5.cloned.1.call-done = f32[13,2048]{1,0:T(8,128)} async-done(((f32[13,2048]{1,0:T(8,128)}), f32[13,2048]{1,0:T(8,128)}) %all-reduce.5.cloned.1.call-update) | async-done | bytes 106512 | tf_op jit(solution)/shard_map/psum | solution.py:78
  221.2 0.9 broadcast_multiply_fusion
  222.1 1.0 multiply_add_fusion.1
  223.1 20.9 %while.21 = (s32[]{:T(128)}, f32[4,6,512]{2,1,0:T(8,128)S(1)}, f32[1024]{0:T(1024)S(1)}, f32[3,1024]{1,0:T(4,128)S(1)}, f32[4,3,512]{2,1,0:T(4,128)S(1)}, /*inde...) while((s32[]{:T(128)}, f32[4,6,512]{2,1,0:T(8,128)S(1)}, f32[1024]{0:T(1024)S(1)}, ...), condition=%wide.region_16.18_spmd, body=%wide.region_11.17_spmd.sunk | while | flops 24117248 | bytes 16924772 | solution.py:44
  223.2 1.8 fusion.34
  225.0 0.9 multiply_divide_fusion.5
  225.9 2.4 fusion.35
  228.4 1.8 fusion.34
  230.2 0.9 multiply_divide_fusion.5
  231.2 2.4 fusion.35
  233.6 1.8 fusion.34
  235.4 0.9 multiply_divide_fusion.5
  236.4 2.4 fusion.35
  238.9 1.8 fusion.34
  240.7 0.9 multiply_divide_fusion.5
  241.6 2.4 fusion.35
  244.1 26.3 %psum.31 = f32[6,2048]{1,0:T(8,128)S(1)} all-reduce(f32[6,2048]{1,0:T(8,128)S(1)} %bitcast.105), channel_id=1, replica_groups=mesh['ia'=4,'ja'=8] {'ja'}, use_global_device_ids=true, to_apply=%region_17.19 | all-reduce | flops 12288 | bytes 98304 | tf_op jit(solution)/shard_map/psum | solution.py:82
  270.6 10.0 %all_gather.15 = f32[12,8192]{1,0:T(8,128)S(1)} all-gather(f32[12,2048]{1,0:T(8,128)S(1)} %pad_maximum_fusion.2), channel_id=1, replica_groups=mesh['ia'=4,'ja'=8] {'ia'}, dimensions={1}, use_global_device_ids=true | all-gather | bytes 491520 | tf_op jit(solution)/shard_map/all_gather | solution.py:90
  280.6 2.6 copy.124
  283.2 21.1 %scatter_fusion.2 = f32[12,1024]{0,1:T(8,128)S(1)} fusion(f32[12,1024]{0,1:T(8,128)S(1)} %scatter_fusion, s32[8192]{0:T(1024)S(1)} %compare_select_fusion, f32[8192,12]{1,0:T(8,128)} %copy.124), kind=kCustom, calls=%fused_computation.4 | custom fusion | bytes 1212416 | tf_op jit(solution)/shard_map/scatter | solution.py:96
  (65 shorter events, 9.3 us)
Async XLA Ops:
  7.2 67.6 %all-reduce.3.cloned.1.call-start = ((), (), s32[]{:S(2)}) async-start(), calls=%async_computation | async-start | bytes 262144 | tf_op jit(solution)/shard_map/psum | solution.py:78
  17.8 203.4 %all-reduce.5.cloned.1.call-start = ((), (), s32[]{:S(2)}) async-start(), calls=%async_computation.1 | async-start | bytes 262144 | tf_op jit(solution)/shard_map/psum | solution.py:78
  35.7 30.5 %copy-start = (f32[12,1024]{1,0:T(8,128)S(1)}, f32[12,1024]{1,0:T(8,128)}, u32[]{:S(2)}) copy-start(f32[12,1024]{1,0:T(8,128)} %param.11) | copy-start | bytes 147460
  35.7 41.0 %copy-start.3 = (f32[1024]{0:T(1024)S(1)}, f32[1024]{0:T(1024)}, u32[]{:S(2)}) copy-start(f32[1024]{0:T(1024)} %param.12) | copy-start | bytes 12292
  76.7 47.3 %copy-start.1 = (f32[13,2048]{1,0:T(8,128)S(1)}, f32[13,2048]{1,0:T(8,128)}, u32[]{:S(2)}) copy-start(f32[13,2048]{1,0:T(8,128)} %all-reduce.3.cloned.1.call-done) | copy-start | bytes 319492
  223.1 47.3 %copy-start.2 = (f32[13,2048]{1,0:T(8,128)S(1)}, f32[13,2048]{1,0:T(8,128)}, u32[]{:S(2)}) copy-start(f32[13,2048]{1,0:T(8,128)} %all-reduce.5.cloned.1.call-done) | copy-start | bytes 319492
Sparse Core Ops, SparseCore 0:
  17.9 56.8 all-reduce.2
  169.4 51.7 all-reduce.4
where the time goes:
time: 313 us
  local copies, waits for them, and re-layouts  98.5 us (31%)
  blocking collectives  90.4 us (29%)
  waiting for transfers between devices  57.9 us (18%)
  other arithmetic  50.9 us (16%)
  between operations  14.3 us (5%)
    psum x2, waiting for transfers between devices, local(): target_state = lax.psum(picked, 'ja')  57.9 us
    psum x2, blocking collectives, local(): forces = lax.psum(partial_value, 'ja')  52.7 us
    scatter x2, local copies, waits for them, and re-layouts, local(): state = state.at[:, placed].set(returned, mode='drop')  42.3 us
    scatter x1, local copies, waits for them, and re-layouts, local(): last = last.at[placed].set(clock, mode='drop')  30.4 us
    all_gather x2, blocking collectives, local(): lax.all_gather(outgoing, 'ia', axis=1, tiled=True)  20 us
    reduce_sum x8, other arithmetic, field_force(): accel = jnp.sum(weight[None] * offset, axis=2)  19.5 us
    all_gather x2, blocking collectives, local(): lax.all_gather(write_ids, 'ia', axis=0, tiled=True)  17.7 us
    gather x4, local copies, waits for them, and re-layouts, local(): picked = jnp.where(inside[None, :], jnp.take(stacked, clipped, axis=1), 0.0)  14.9 us
  transfers between devices with their start and end apart: 2, of which 2 were waited for; matrix products, arithmetic and copies ran while one was open for 11% of the time, Pallas kernels for 0%

commit v1 on v0

--- a/solution.py
+++ b/solution.py
@@ -79,7 +79,7 @@
         tpos, tvel = predict(target_state[0:12], clock - target_state[12])
         partial_value = blocked_force(tpos, tvel, fpos, fvel, star_mass, block_rows)
         write_ids = jnp.where(usable, indices, -1)
-        forces = lax.psum(partial_value, "ja")
+        forces = jnp.sum(lax.all_gather(partial_value, "ja"), axis=0)
         share_len = forces.shape[1] // lax.axis_size("ja")
         share_start = lax.axis_index("ja") * share_len
         force_share = lax.dynamic_slice_in_dim(forces, share_start, share_len, 1)

time: 313 us -> 292 us (0.933)
  blocking collectives: 90.4 us -> 68.1 us
    psum x2 -> x0, blocking collectives: 52.7 us -> none  [local(): forces = lax.psum(partial_value, 'ja')]
    all_gather x0 -> x2, blocking collectives: none -> 29.7 us  [local(): forces = jnp.sum(lax.all_gather(partial_value, 'ja'), axis=0)]
where the time goes in v1:
time: 292 us; the launch traced here: 291 us
  local copies, waits for them, and re-layouts  98.5 us (34%)
  blocking collectives  68.1 us (23%)
  waiting for transfers between devices  58.7 us (20%)
  other arithmetic  51 us (17%)
  between operations  14.3 us (5%)
    psum x2, waiting for transfers between devices, local(): target_state = lax.psum(picked, 'ja')  58.7 us
    scatter x2, local copies, waits for them, and re-layouts, local(): state = state.at[:, placed].set(returned, mode='drop')  42.3 us
    scatter x1, local copies, waits for them, and re-layouts, local(): last = last.at[placed].set(clock, mode='drop')  30.4 us
    all_gather x2, blocking collectives, local(): forces = jnp.sum(lax.all_gather(partial_value, 'ja'), axis=0)  29.7 us
    all_gather x2, blocking collectives, local(): lax.all_gather(outgoing, 'ia', axis=1, tiled=True)  20.7 us
    reduce_sum x8, other arithmetic, field_force(): accel = jnp.sum(weight[None] * offset, axis=2)  19.5 us
    all_gather x2, blocking collectives, local(): lax.all_gather(write_ids, 'ia', axis=0, tiled=True)  17.7 us
    gather x4, local copies, waits for them, and re-layouts, local(): picked = jnp.where(inside[None, :], jnp.take(stacked, clipped, axis=1), 0.0)  14.9 us
  transfers between devices with their start and end apart: 2, of which 2 were waited for; matrix products, arithmetic and copies ran while one was open for 11% of the time, Pallas kernels for 0%

profile of v1, /device:TPU:0, one launch (start us, length us, event | category | flops | bytes accessed | tf_op | source)
XLA Modules:
  0.0 291.1 jit_solution(2669208929478808065)
XLA Ops:
  11.3 5.5 %gather_fusion = f32[2048,13]{1,0:T(8,128)S(1)} fusion(f32[13,1024]{0,1:T(8,128)S(1)} %copy.141, s32[2048]{0:T(1024)S(1)} %get-tuple-element.166), kind=kCustom, calls=%fused_computation.clone | custom fusion | bytes 221184 | tf_op jit(solution)/shard_map/jit(_take)/gather | solution.py:77
  17.9 9.6 %all_gather.21 = s32[8192]{0:T(1024)S(1)} all-gather(s32[2048]{0:T(1024)S(1)} %get-tuple-element.167), channel_id=1, replica_groups=mesh['ia'=4,'ja'=8] {'ia'}, dimensions={0}, use_global_device_ids=true | all-gather | bytes 40960 | tf_op jit(solution)/shard_map/all_gather | solution.py:91
  27.5 8.1 %all_gather.18 = s32[8192]{0:T(1024)S(1)} all-gather(s32[2048]{0:T(1024)S(1)} %get-tuple-element.168), channel_id=1, replica_groups=mesh['ia'=4,'ja'=8] {'ia'}, dimensions={0}, use_global_device_ids=true | all-gather | bytes 40960 | tf_op jit(solution)/shard_map/all_gather | solution.py:91
  35.7 30.4 %scatter_fusion.1 = f32[1024]{0:T(1024)S(1)} fusion(f32[1024]{0:T(1024)S(1)} %get-tuple-element.172, s32[8192]{0:T(1024)S(1)} %compare_select_fusion.1, f32[8192]{0:T(1024)S(1)} %broadcast.175), kind=kCustom, calls=%fused_computation.3 | custom fusion | bytes 131072 | tf_op jit(solution)/shard_map/scatter | solution.py:97
  66.9 7.9 %all-reduce.3.cloned.1.call-done = f32[13,2048]{1,0:T(8,128)} async-done(((f32[13,2048]{1,0:T(8,128)}), f32[13,2048]{1,0:T(8,128)}) %all-reduce.3.cloned.1.call-update) | async-done | bytes 106512 | tf_op jit(solution)/shard_map/psum | solution.py:78
  74.8 0.9 broadcast_multiply_fusion.1
  75.7 1.0 multiply_add_fusion.4
  76.8 20.9 %while.20 = (s32[]{:T(128)}, f32[4,6,512]{2,1,0:T(8,128)S(1)}, f32[1024]{0:T(1024)S(1)}, f32[3,1024]{1,0:T(4,128)S(1)}, f32[4,3,512]{2,1,0:T(4,128)S(1)}, /*inde...) while((s32[]{:T(128)}, f32[4,6,512]{2,1,0:T(8,128)S(1)}, f32[1024]{0:T(1024)S(1)}, ...), condition=%wide.region_6.8_spmd, body=%wide.region_1.7_spmd.sunk | while | flops 24117248 | bytes 16924772 | solution.py:44
  76.8 1.8 fusion.31
  78.6 0.9 multiply_divide_fusion.4
  79.5 2.4 fusion.32
  82.0 1.8 fusion.31
  83.8 0.9 multiply_divide_fusion.4
  84.8 2.4 fusion.32
  87.2 1.8 fusion.31
  89.0 0.9 multiply_divide_fusion.4
  90.0 2.4 fusion.32
  92.5 1.8 fusion.31
  94.3 0.9 multiply_divide_fusion.4
  95.2 2.4 fusion.32
  97.7 14.8 %all_gather.19 = f32[8,6,2048]{2,1,0:T(8,128)S(1)} all-gather(f32[1,6,2048]{2,1,0:T(8,128)S(1)} %bitcast.105), channel_id=1, replica_groups=mesh['ia'=4,'ja'=8] {'ja'}, dimensions={0}, use_global_device_ids=true | all-gather | bytes 442368 | tf_op jit(solution)/shard_map/all_gather | solution.py:82
  112.7 10.3 %all_gather.20 = f32[12,8192]{1,0:T(8,128)S(1)} all-gather(f32[12,2048]{1,0:T(8,128)S(1)} %pad_maximum_fusion.1), channel_id=1, replica_groups=mesh['ia'=4,'ja'=8] {'ia'}, dimensions={1}, use_global_device_ids=true | all-gather | bytes 491520 | tf_op jit(solution)/shard_map/all_gather | solution.py:90
  123.0 2.6 copy.146
  125.6 21.2 %scatter_fusion = f32[12,1024]{0,1:T(8,128)S(1)} fusion(f32[12,1024]{0,1:T(8,128)S(1)} %copy.145, s32[8192]{0:T(1024)S(1)} %compare_select_fusion.1, f32[8192,12]{1,0:T(8,128)} %copy.146), kind=kCustom, calls=%fused_computation.2 | custom fusion | bytes 1212416 | tf_op jit(solution)/shard_map/scatter | solution.py:96
  146.9 1.3 fusion.24
  148.4 7.6 %gather_fusion.1 = f32[2048,13]{1,0:T(8,128)} fusion(f32[13,1024]{0,1:T(8,128)S(1)} %pad_maximum_fusion, s32[2048]{0:T(1024)S(1)} %get-tuple-element.165), kind=kCustom, calls=%fused_computation.1.clone | custom fusion | bytes 221184 | tf_op jit(solution)/shard_map/jit(_take)/gather | solution.py:77
  155.9 1.6 copy.148
  158.2 1.2 copy.160
  160.1 50.8 %all-reduce.5.cloned.1.call-done = f32[13,2048]{1,0:T(8,128)} async-done(((f32[13,2048]{1,0:T(8,128)}), f32[13,2048]{1,0:T(8,128)}) %all-reduce.5.cloned.1.call-update) | async-done | bytes 106512 | tf_op jit(solution)/shard_map/psum | solution.py:78
  210.9 0.9 broadcast_multiply_fusion
  211.7 1.0 multiply_add_fusion.1
  212.8 20.9 %while.21 = (s32[]{:T(128)}, f32[4,6,512]{2,1,0:T(8,128)S(1)}, f32[1024]{0:T(1024)S(1)}, f32[3,1024]{1,0:T(4,128)S(1)}, f32[4,3,512]{2,1,0:T(4,128)S(1)}, /*inde...) while((s32[]{:T(128)}, f32[4,6,512]{2,1,0:T(8,128)S(1)}, f32[1024]{0:T(1024)S(1)}, ...), condition=%wide.region_16.18_spmd, body=%wide.region_11.17_spmd.sunk | while | flops 24117248 | bytes 16924772 | solution.py:44
  212.8 1.8 fusion.34
  214.6 0.9 multiply_divide_fusion.5
  215.6 2.4 fusion.35
  218.1 1.8 fusion.34
  219.9 0.9 multiply_divide_fusion.5
  220.8 2.4 fusion.35
  223.3 1.8 fusion.34
  225.1 0.9 multiply_divide_fusion.5
  226.0 2.4 fusion.35
  228.5 1.8 fusion.34
  230.3 0.9 multiply_divide_fusion.5
  231.3 2.4 fusion.35
  233.7 14.8 %all_gather.22 = f32[8,6,2048]{2,1,0:T(8,128)S(1)} all-gather(f32[1,6,2048]{2,1,0:T(8,128)S(1)} %bitcast.106), channel_id=1, replica_groups=mesh['ia'=4,'ja'=8] {'ja'}, dimensions={0}, use_global_device_ids=true | all-gather | bytes 442368 | tf_op jit(solution)/shard_map/all_gather | solution.py:82
  248.8 10.3 %all_gather.23 = f32[12,8192]{1,0:T(8,128)S(1)} all-gather(f32[12,2048]{1,0:T(8,128)S(1)} %pad_maximum_fusion.2), channel_id=1, replica_groups=mesh['ia'=4,'ja'=8] {'ia'}, dimensions={1}, use_global_device_ids=true | all-gather | bytes 491520 | tf_op jit(solution)/shard_map/all_gather | solution.py:90
  259.1 2.6 copy.155
  261.7 21.1 %scatter_fusion.2 = f32[12,1024]{0,1:T(8,128)S(1)} fusion(f32[12,1024]{0,1:T(8,128)S(1)} %scatter_fusion, s32[8192]{0:T(1024)S(1)} %compare_select_fusion, f32[8192,12]{1,0:T(8,128)} %copy.155), kind=kCustom, calls=%fused_computation.4 | custom fusion | bytes 1212416 | tf_op jit(solution)/shard_map/scatter | solution.py:96
  (67 shorter events, 9.4 us)
Async XLA Ops:
  7.2 67.6 %all-reduce.3.cloned.1.call-start = ((), (), s32[]{:S(2)}) async-start(), calls=%async_computation | async-start | bytes 262144 | tf_op jit(solution)/shard_map/psum | solution.py:78
  17.8 193.1 %all-reduce.5.cloned.1.call-start = ((), (), s32[]{:S(2)}) async-start(), calls=%async_computation.1 | async-start | bytes 262144 | tf_op jit(solution)/shard_map/psum | solution.py:78
  35.7 30.5 %copy-start = (f32[12,1024]{1,0:T(8,128)S(1)}, f32[12,1024]{1,0:T(8,128)}, u32[]{:S(2)}) copy-start(f32[12,1024]{1,0:T(8,128)} %param.11) | copy-start | bytes 147460
  35.7 41.0 %copy-start.3 = (f32[1024]{0:T(1024)S(1)}, f32[1024]{0:T(1024)}, u32[]{:S(2)}) copy-start(f32[1024]{0:T(1024)} %param.12) | copy-start | bytes 12292
  76.7 35.8 %copy-start.1 = (f32[13,2048]{1,0:T(8,128)S(1)}, f32[13,2048]{1,0:T(8,128)}, u32[]{:S(2)}) copy-start(f32[13,2048]{1,0:T(8,128)} %all-reduce.3.cloned.1.call-done) | copy-start | bytes 319492
  212.8 35.9 %copy-start.2 = (f32[13,2048]{1,0:T(8,128)S(1)}, f32[13,2048]{1,0:T(8,128)}, u32[]{:S(2)}) copy-start(f32[13,2048]{1,0:T(8,128)} %all-reduce.5.cloned.1.call-done) | copy-start | bytes 319492
Sparse Core Ops, SparseCore 0:
  17.9 56.8 all-reduce.2
  158.3 52.5 all-reduce.4
